TPU v7x, 32 devices: a whole 2x2x4 slice. The times are simulated.
32 devices in a mesh: flow: 8 (over z, y), group: 4 (over x, core).
Axes of the slice: x: 2, y: 2, z: 4, core: 2. Of those that a mesh axis runs over, the one named last changes fastest.
Arguments:
- cell_state: float32 [12, 262144], P(None, 'flow'), may hold values from 0.1 to 10
- inflow: float32 [12, 2048], P(None, ('flow', 'group')), may hold values from 0.1 to 10
- courant: float32 [256, 2048], P(None, ('flow', 'group')), may hold values from 1 to 15360
- pick: int32 [4, 8, 8, 2048], P('group', 'flow'), may hold values from 0 to 32767, as said below
- node_slot: int32 [256, 2048], P(None, ('flow', 'group')), may hold values from 0 to 16383, as said below
- stoich: float32 [6, 12], replicated, may hold values from 0 to 0.25
- logk: float32 [6], replicated, may hold values from -3 to 0
Outputs:
- cell_species: float32 [18, 262144], P(None, ('flow', 'group'))
Inputs may be any that keep to these rules, and one draw needn't show every extreme that they name: pick[g, a, b, k] lies in the block of 128 local cells numbered ((b * 2048 + k) // 128 + g * 128) modulo (256). With j = s % 64, node_slot[n, s] lies in the tile of 128 records numbered (n * 64 + j) // 128.
All inputs are finite; a program needn't handle non-finite values.
Results may differ from a plain program's by a relative error of at most 0.00011.
Values sent between devices are 32-bit elements; how exact they have to be, the bound alone decides.
A program may use at most 128 MiB of HBM per device.

v0:
```python
import jax
import jax.numpy as jnp
from jax import lax
from jax.sharding import PartitionSpec as P

ITERS = 4
WIN = 128


def solve_spd(matrix, rhs):
    order = len(rhs)
    lower = {}
    inverse = []
    for outer in range(order):
        for inner in range(outer + 1):
            total = matrix[outer, inner]
            for other in range(inner):
                total = total - lower[outer, other] * lower[inner, other]
            if outer == inner:
                inverse.append(lax.rsqrt(total))
            else:
                lower[outer, inner] = total * inverse[inner]
    middle = []
    for outer in range(order):
        total = rhs[outer]
        for other in range(outer):
            total = total - lower[outer, other] * middle[other]
        middle.append(total * inverse[outer])
    result = [None] * order
    for outer in reversed(range(order)):
        total = middle[outer]
        for other in range(outer + 1, order):
            total = total - lower[other, outer] * result[other]
        result[outer] = total * inverse[outer]
    return result


def speciate(totals, stoich, logk):
    count_comp = totals.shape[0]
    identity = jnp.eye(count_comp, dtype=jnp.float32)
    logfree = jnp.log(totals)
    for sweep in range(ITERS):
        free = jnp.exp(logfree)
        complexes = jnp.exp(
            logk[:, None]
            + jnp.dot(
                stoich, logfree, precision=lax.Precision.HIGHEST, preferred_element_type=jnp.float32
            )
        )
        mismatch = (
            free
            + jnp.dot(
                stoich.T,
                complexes,
                precision=lax.Precision.HIGHEST,
                preferred_element_type=jnp.float32,
            )
            - totals
        )
        jacobian = jnp.einsum(
            "pi,pj,pn->ijn", stoich, stoich, complexes, precision=lax.Precision.HIGHEST
        )
        jacobian = jacobian + identity[:, :, None] * free[:, None, :]
        update = solve_spd(jacobian, [-mismatch[comp] for comp in range(count_comp)])
        logfree = logfree + jnp.stack(update)
    complexes = jnp.exp(
        logk[:, None]
        + jnp.dot(
            stoich, logfree, precision=lax.Precision.HIGHEST, preferred_element_type=jnp.float32
        )
    )
    return jnp.concatenate([jnp.exp(logfree), complexes], axis=0)


def compose_nodes(earlier, later):
    return (later[0] * earlier[0], later[0][:, None, :] * earlier[1] + later[1])


def one_hot_tiles(local, window):
    positions = lax.broadcasted_iota(jnp.int32, (1, window, 1), 1)
    return (local[:, None, :] == positions).astype(jnp.float32)


def body(cell_state, inflow, courant, pick, node_slot, stoich, logk):
    count_comp, cell_count = cell_state.shape
    node_count, lines = courant.shape
    flow_count = lax.axis_size("flow")
    capacity = pick.shape[3]
    slot_total = flow_count * capacity
    tile_count = slot_total // WIN
    block_count = cell_count // WIN
    used = min(tile_count, block_count)
    repeat = tile_count // used
    offset = lax.axis_index("group") * tile_count % block_count
    pick_table = one_hot_tiles(pick.reshape(tile_count, WIN) % WIN, WIN)
    node_table = one_hot_tiles(node_slot.reshape(tile_count, WIN) % WIN, WIN)
    cell_blocks = cell_state.reshape(count_comp, block_count, WIN)
    doubled = jnp.concatenate([cell_blocks, cell_blocks], axis=1)
    chosen = lax.dynamic_slice_in_dim(doubled, offset, used, 1)
    chosen = jnp.tile(chosen, (1, repeat, 1))
    outgoing = jnp.einsum("ctl,tlr->ctr", chosen, pick_table, precision=lax.Precision.HIGHEST)
    incoming = lax.all_to_all(
        outgoing.reshape(count_comp, flow_count, capacity),
        "flow",
        split_axis=1,
        concat_axis=1,
        tiled=True,
    )
    records = incoming.reshape(count_comp, tile_count, WIN)
    old = jnp.einsum("ctl,tln->ctn", records, node_table, precision=lax.Precision.HIGHEST)
    old = old.reshape(count_comp, node_count, lines)
    weight = courant / (1.0 + courant)
    source = jnp.transpose(old / (1.0 + courant)[None], (1, 0, 2))
    running_scale, running_offset = lax.associative_scan(compose_nodes, (weight, source), axis=0)
    moved = running_scale[:, None, :] * inflow[None] + running_offset
    moved = jnp.transpose(moved, (1, 0, 2)).reshape(count_comp, node_count * lines)
    species = speciate(moved, stoich, logk)
    width = species.shape[0]
    species_tiles = species.reshape(width, tile_count, WIN)
    slot_sums = jnp.einsum(
        "qtn,tln->qtl", species_tiles, node_table, precision=lax.Precision.HIGHEST
    )
    slot_counts = jnp.sum(node_table, axis=2)[None]
    back_sums, back_counts = (
        lax.all_to_all(
            slot_sums.reshape(width, flow_count, capacity),
            "flow",
            split_axis=1,
            concat_axis=1,
            tiled=True,
        ),
        lax.all_to_all(
            slot_counts.reshape(1, flow_count, capacity),
            "flow",
            split_axis=1,
            concat_axis=1,
            tiled=True,
        ),
    )
    returned = jnp.concatenate(
        [back_sums.reshape(width, tile_count, WIN), back_counts.reshape(1, tile_count, WIN)], axis=0
    )
    placed = jnp.einsum("qtr,tlr->qtl", returned, pick_table, precision=lax.Precision.HIGHEST)
    placed = jnp.sum(placed.reshape(width + 1, repeat, used, WIN), axis=1)
    buffer = jnp.zeros((width + 1, 2 * block_count, WIN), jnp.float32)
    buffer = lax.dynamic_update_slice_in_dim(buffer, placed, offset, 1)
    folded = (buffer[:, :block_count] + buffer[:, block_count:]).reshape(width + 1, cell_count)
    cell_sums = folded[:width]
    cell_counts = folded[width:]
    full_sums, full_counts = lax.psum((cell_sums, cell_counts), "group")
    block = cell_count // lax.axis_size("group")
    begin = lax.axis_index("group") * block
    own_sums = lax.dynamic_slice_in_dim(full_sums, begin, block, 1)
    own_counts = lax.dynamic_slice_in_dim(full_counts, begin, block, 1)
    return own_sums / jnp.maximum(own_counts, 1.0)


def solution(mesh):
    placed = (
        P(None, "flow"),
        P(None, ("flow", "group")),
        P(None, ("flow", "group")),
        P("group", "flow", None, None),
        P(None, ("flow", "group")),
        P(),
        P(),
    )
    return jax.shard_map(
        body, mesh=mesh, in_specs=placed, out_specs=P(None, ("flow", "group")), check_vma=False
    )
```

profile of v0, /device:TPU:0, one launch (start us, length us, event | category | flops | bytes accessed | tf_op | source)
XLA Modules:
  0.0 417.0 jit_solution(14318310937043058263)
XLA Ops:
  10.5 4.1 fusion.36
  16.6 7.7 %all-to-all-start = ((f32[12,8,2048]{2,0,1:T(8,128)}), f32[12,8,2048]{2,0,1:T(8,128)S(1)}, u32[]{:S(2)}, u32[]{:S(2)}) async-start(f32[12,8,2048]{2,0,1:T(8,128)} %copy.60), calls=%async_computation | async-start | bytes 2097152 | tf_op jit(solution)/shard_map/all_to_all | solution.py:102
  29.2 20.7 %all-to-all-done = f32[12,8,2048]{2,0,1:T(8,128)S(1)} async-done(((f32[12,8,2048]{2,0,1:T(8,128)}), f32[12,8,2048]{2,0,1:T(8,128)S(1)}, u32[]{:S(2)}, u32[]{:S(2)}) %all-to-all-start) | async-done | bytes 786464 | tf_op jit(solution)/shard_map/all_to_all | solution.py:102
  50.6 4.1 fusion.37
  70.8 5.3 %pad.129 = f32[256,12,64]{2,0,1:T(8,128)S(1)} pad(f32[128,12,64]{2,0,1:T(8,128)} %add.328, f32[]{:T(128)} %constant.38.clone.1), padding=1_0_1x0_0_0x0_0_0 | pad | bytes 1179652 | tf_op jit(solution)/shard_map/pad | solution.py:114
  78.4 5.8 %pad.128 = f32[256,12,64]{2,0,1:T(8,128)S(1)} pad(f32[128,12,64]{2,0,1:T(8,128)} %pad_maximum_fusion.1, f32[]{:T(128)} %constant.38.clone.1), padding=0_1_1x0_0_0x0_0_0 | pad | bytes 1179652 | tf_op jit(solution)/shard_map/pad | solution.py:114
  89.9 12.8 %fusion = f32[12,12,16384]{2,0,1:T(8,128)S(1)} fusion(f32[12,16384]{1,0:T(8,128)S(1)} %log_exponential_fusion, f32[12,12]{0,1:T(8,128)S(1)} %copy-done.9, f32[16384,6]{0,1:T(8,128)S(1)} %fusion.17, f32[6,12]{1,0:T(8,128)S(1)} %copy-done, f32[6,12]{0,1:T(8,128)S(1)} %copy.64), kind=kOutput, calls=%fused_computation.4 | convolution fusion | flops 174588768 | bytes 10617984 | tf_op jit(solution)/shard_map/pi,pj,pn->ijn/dot_general | solution.py:60
  102.8 13.7 %subtract_multiply_fusion.159 = (f32[1,16384]{1,0:T(1,128)S(1)}, f32[1,16384]{1,0:T(1,128)S(1)}, f32[1,16384]{1,0:T(1,128)S(1)}, f32[1,16384]{1,0:T(1,128)S(1)},...) fusion(f32[12,16384]{1,0:T(8,128)S(1)} %fusion.11, ...), kind=kLoop, calls=%fused_computation.1528 | loop fusion | flops 10272768 | bytes 9830400 | tf_op jit(solution)/shard_map/mul | solution.py:28
  116.5 4.4 %subtract_multiply_fusion.152 = (f32[1,16384]{1,0:T(1,128)S(1)}, f32[1,16384]{1,0:T(1,128)S(1)}, f32[1,16384]{1,0:T(1,128)S(1)}, f32[1,16384]{1,0:T(1,128)S(1)},...) fusion(f32[1,16384]{1,0:T(1,128)S(1)} %get-tuple-element.322, ...), kind=kLoop, calls=%fused_computation.1520 | loop fusion | flops 2310144 | bytes 5767168 | tf_op jit(solution)/shard_map/mul | solution.py:22
  120.9 6.5 %subtract_multiply_fusion.141 = (f32[1,16384]{1,0:T(1,128)}, f32[1,16384]{1,0:T(1,128)}, f32[1,16384]{1,0:T(1,128)}, f32[1,16384]{1,0:T(1,128)}, f32[1,16384]{1,...) fusion(f32[1,16384]{1,0:T(1,128)S(1)} %get-tuple-element.394, ...), kind=kLoop, calls=%fused_computation.1509 | loop fusion | flops 3440640 | bytes 6684672 | tf_op jit(solution)/shard_map/mul | solution.py:34
  132.8 12.8 %fusion.1 = f32[12,12,16384]{2,0,1:T(8,128)S(1)} fusion(f32[12,16384]{1,0:T(8,128)S(1)} %fusion.1002, f32[12,12]{0,1:T(8,128)S(1)} %copy-done.10, f32[16384,6]{0,1:T(8,128)S(1)} %fusion.16, f32[6,12]{1,0:T(8,128)S(1)} %copy-done, f32[6,12]{0,1:T(8,128)S(1)} %copy.64), kind=kOutput, calls=%fused_computation.5 | convolution fusion | flops 174588768 | bytes 10617984 | tf_op jit(solution)/shard_map/pi,pj,pn->ijn/dot_general | solution.py:60
  145.6 13.8 %subtract_multiply_fusion.112 = (f32[1,16384]{1,0:T(1,128)S(1)}, f32[1,16384]{1,0:T(1,128)S(1)}, f32[1,16384]{1,0:T(1,128)S(1)}, f32[1,16384]{1,0:T(1,128)S(1)},...) fusion(f32[12,16384]{1,0:T(8,128)S(1)} %fusion.9, ...), kind=kLoop, calls=%fused_computation.1474 | loop fusion | flops 10272768 | bytes 9830400 | tf_op jit(solution)/shard_map/mul | solution.py:28
  159.4 4.2 subtract_multiply_fusion.105
  163.6 6.5 %subtract_multiply_fusion.94 = (f32[1,16384]{1,0:T(1,128)}, f32[1,16384]{1,0:T(1,128)}, f32[1,16384]{1,0:T(1,128)}, f32[1,16384]{1,0:T(1,128)}, f32[1,16384]{1,0...) fusion(f32[1,16384]{1,0:T(1,128)S(1)} %get-tuple-element.298, ...), kind=kLoop, calls=%fused_computation.1455 | loop fusion | flops 3440640 | bytes 6684672 | tf_op jit(solution)/shard_map/mul | solution.py:34
  170.1 4.6 %stack.9 = f32[12,16384]{1,0:T(8,128)} concatenate(f32[1,16384]{1,0:T(1,128)} %get-tuple-element.203, f32[1,16384]{1,0:T(1,128)} %get-tuple-element.204, f32[1,16384]{1,0:T(1,128)} %get-tuple-element.205, f32[1,16384]{1,0:T(1,128)} %get-tuple-element.206, f32[1,16384]{1,0:T(1,128)} %get-tuple-element.207, f32[1,16384]{1,0:T(1,128)} %get-tuple-element.208, ...), dimensions={0} | concatenate | bytes 1572864 | tf_op jit(solution)/shard_map/stack | solution.py:65
  178.1 12.8 %fusion.2 = f32[12,12,16384]{2,0,1:T(8,128)S(1)} fusion(f32[12,16384]{1,0:T(8,128)S(1)} %get-tuple-element.201, f32[12,12]{0,1:T(8,128)S(1)} %copy-done.11, f32[16384,6]{0,1:T(8,128)S(1)} %fusion.15, f32[6,12]{1,0:T(8,128)S(1)} %copy-done, f32[6,12]{0,1:T(8,128)S(1)} %copy.64), kind=kOutput, calls=%fused_computation.6 | convolution fusion | flops 174588768 | bytes 10617984 | tf_op jit(solution)/shard_map/pi,pj,pn->ijn/dot_general | solution.py:60
  190.9 13.9 %subtract_multiply_fusion.65 = (f32[1,16384]{1,0:T(1,128)S(1)}, f32[1,16384]{1,0:T(1,128)S(1)}, f32[1,16384]{1,0:T(1,128)S(1)}, f32[1,16384]{1,0:T(1,128)S(1)}, ...) fusion(f32[12,16384]{1,0:T(8,128)S(1)} %fusion.7, ...), kind=kLoop, calls=%fused_computation.1420 | loop fusion | flops 10272768 | bytes 9830400 | tf_op jit(solution)/shard_map/mul | solution.py:28
  204.8 4.1 subtract_multiply_fusion.58
  209.0 6.5 %subtract_multiply_fusion.47 = (f32[1,16384]{1,0:T(1,128)}, f32[1,16384]{1,0:T(1,128)}, f32[1,16384]{1,0:T(1,128)}, f32[1,16384]{1,0:T(1,128)}, f32[1,16384]{1,0...) fusion(f32[1,16384]{1,0:T(1,128)S(1)} %get-tuple-element.200, ...), kind=kLoop, calls=%fused_computation.1401 | loop fusion | flops 3440640 | bytes 6684672 | tf_op jit(solution)/shard_map/mul | solution.py:34
  215.5 4.2 %stack.10 = f32[12,16384]{1,0:T(8,128)} concatenate(f32[1,16384]{1,0:T(1,128)} %get-tuple-element.105, f32[1,16384]{1,0:T(1,128)} %get-tuple-element.106, f32[1,16384]{1,0:T(1,128)} %get-tuple-element.107, f32[1,16384]{1,0:T(1,128)} %get-tuple-element.108, f32[1,16384]{1,0:T(1,128)} %get-tuple-element.109, f32[1,16384]{1,0:T(1,128)} %get-tuple-element.110, ...), dimensions={0} | concatenate | bytes 1572864 | tf_op jit(solution)/shard_map/stack | solution.py:65
  223.0 13.0 %fusion.3 = f32[12,12,16384]{2,0,1:T(8,128)S(1)} fusion(f32[12,16384]{1,0:T(8,128)S(1)} %get-tuple-element.103, f32[12,12]{0,1:T(8,128)S(1)} %copy-done.12, f32[16384,6]{0,1:T(8,128)S(1)} %fusion.14, f32[6,12]{1,0:T(8,128)S(1)} %copy-done, f32[6,12]{0,1:T(8,128)S(1)} %copy.64), kind=kOutput, calls=%fused_computation.7 | convolution fusion | flops 174588768 | bytes 10617984 | tf_op jit(solution)/shard_map/pi,pj,pn->ijn/dot_general | solution.py:60
  236.0 13.8 %subtract_multiply_fusion.18 = (f32[1,16384]{1,0:T(1,128)S(1)}, f32[1,16384]{1,0:T(1,128)S(1)}, f32[1,16384]{1,0:T(1,128)S(1)}, f32[1,16384]{1,0:T(1,128)S(1)}, ...) fusion(f32[12,16384]{1,0:T(8,128)S(1)} %fusion.5, ...), kind=kLoop, calls=%fused_computation.1366 | loop fusion | flops 10272768 | bytes 9830400 | tf_op jit(solution)/shard_map/mul | solution.py:28
  249.8 4.2 subtract_multiply_fusion.11
  253.9 6.5 %subtract_multiply_fusion = (f32[1,16384]{1,0:T(1,128)}, f32[1,16384]{1,0:T(1,128)}, f32[1,16384]{1,0:T(1,128)}, f32[1,16384]{1,0:T(1,128)}, f32[1,16384]{1,0:T(...) fusion(f32[1,16384]{1,0:T(1,128)S(1)} %get-tuple-element.102, ...), kind=kLoop, calls=%fused_computation.1347 | loop fusion | flops 3440640 | bytes 6684672 | tf_op jit(solution)/shard_map/mul | solution.py:34
  265.6 6.6 %fusion.30 = f32[18,128,128]{2,0,1:T(8,128)S(1)} fusion(f32[18,128,128]{2,1,0:T(8,128)S(1)} %slice.2170, s32[128,128]{1,0:T(8,128)S(1)} %copy-done.8), kind=kOutput, calls=%fused_computation.52 | convolution fusion | flops 455081984 | bytes 2424832 | tf_op jit(solution)/shard_map/qtn,tln->qtl/dot_general | solution.py:120
  274.5 3.6 all-to-all-start.1
  280.1 35.2 %all-to-all-done.1 = f32[18,8,2048]{2,0,1:T(8,128)S(1)} async-done(((f32[18,8,2048]{2,0,1:T(8,128)}), f32[18,8,2048]{2,0,1:T(8,128)S(1)}, u32[]{:S(2)}, u32[]{:S(2)}) %all-to-all-start.1) | async-done | bytes 1179680 | tf_op jit(solution)/shard_map/all_to_all | solution.py:125
  315.3 3.6 all-to-all-start.2
  320.9 5.0 %all-to-all-done.2 = f32[1,8,2048]{2,0,1:T(1,128)S(1)} async-done(((f32[1,8,2048]{2,0,1:T(1,128)}), f32[1,8,2048]{2,0,1:T(1,128)S(1)}, u32[]{:S(2)}, u32[]{:S(2)}) %all-to-all-start.2) | async-done | bytes 65568 | tf_op jit(solution)/shard_map/all_to_all | solution.py:132
  325.9 6.6 %fusion.33 = f32[19,128,128]{2,0,1:T(8,128)S(1)} fusion(f32[1,128,128]{2,0,1:T(1,128)S(1)} %bitcast.3483, f32[18,128,128]{2,0,1:T(8,128)S(1)} %copy.69, s32[128,128]{1,0:T(8,128)S(1)} %copy-done.22), kind=kOutput, calls=%fused_computation.53 | convolution fusion | flops 480559104 | bytes 2555904 | tf_op jit(solution)/shard_map/qtr,tlr->qtl/dot_general | solution.py:143
  334.9 3.5 copy.75
  338.5 68.4 %all-reduce.35.cloned.1.call-done = (f32[18,32768]{1,0:T(8,128)}, f32[1,32768]{1,0:T(1,128)}) async-done(((f32[18,32768]{1,0:T(8,128)}, f32[1,32768]{1,0:T(1,128)}), (f32[18,32768]{1,0:T(8,128)}, f32[1,32768]{1,0:T(1,128)})) %all-reduce.35.cloned.1.call-update) | async-done | bytes 2490384 | tf_op jit(solution)/shard_map/psum | solution.py:150
  (267 shorter events, 63.1 us)
Async XLA Ops:
  7.4 3.1 copy-start.21
  15.0 9.3 %copy-start.19 = (f32[256,64]{0,1:T(8,128)S(1)}, f32[256,64]{0,1:T(8,128)}, u32[]{:S(2)}) copy-start(f32[256,64]{0,1:T(8,128)} %param.9) | copy-start | bytes 196612
  16.6 11.0 %copy-start.20 = (s32[256,64]{0,1:T(8,128)S(1)}, s32[256,64]{0,1:T(8,128)}, u32[]{:S(2)}) copy-start(s32[256,64]{0,1:T(8,128)} %param.11) | copy-start | bytes 196612
  16.6 33.4 %all-to-all-start = ((f32[12,8,2048]{2,0,1:T(8,128)}), f32[12,8,2048]{2,0,1:T(8,128)S(1)}, u32[]{:S(2)}, u32[]{:S(2)}) async-start(f32[12,8,2048]{2,0,1:T(8,128)} %copy.60), calls=%async_computation | async-start | bytes 2097152 | tf_op jit(solution)/shard_map/all_to_all | solution.py:102
  24.3 3.6 copy-start
  24.5 2.9 copy-start.4
  24.6 2.4 copy-start.13
  24.6 2.1 copy-start.16
  24.7 2.2 copy-start.23
  25.3 1.4 copy-start.30
  25.3 1.5 copy-start.26
  25.4 1.4 copy-start.17
  26.9 23.7 %copy-start.1 = (f32[127,64]{1,0:T(8,128)}, f32[127,64]{1,0:T(8,128)S(1)}, u32[]{:S(2)}) copy-start(f32[127,64]{1,0:T(8,128)S(1)} %slice.1329) | copy-start | bytes 97540
  29.2 25.4 %copy-start.7 = (s32[128,128]{1,0:T(8,128)}, s32[128,128]{1,0:T(8,128)S(1)}, u32[]{:S(2)}) copy-start(s32[128,128]{1,0:T(8,128)S(1)} %add_select_fusion) | copy-start | bytes 196612
  60.4 6.9 %copy-start.31 = (f32[2,64]{1,0:T(2,128)S(1)}, f32[2,64]{1,0:T(2,128)}, u32[]{:S(2)}) copy-start(f32[2,64]{1,0:T(2,128)} %copy-done.30) | copy-start | bytes 1540
  60.5 6.9 %copy-start.34 = (f32[64]{0:T(128)S(1)}, f32[64]{0:T(128)}, u32[]{:S(2)}) copy-start(f32[64]{0:T(128)} %get-tuple-element.405) | copy-start | bytes 772
  60.5 7.1 %copy-start.33 = (f32[64]{0:T(128)S(1)}, f32[64]{0:T(128)}, u32[]{:S(2)}) copy-start(f32[64]{0:T(128)} %get-tuple-element.402) | copy-start | bytes 772
  61.2 6.6 %copy-start.27 = (f32[3,64]{1,0:T(4,128)S(1)}, f32[3,64]{1,0:T(4,128)}, u32[]{:S(2)}) copy-start(f32[3,64]{1,0:T(4,128)} %copy-done.26) | copy-start | bytes 2308
  62.8 5.5 %copy-start.18 = (f32[15,64]{1,0:T(8,128)S(1)}, f32[15,64]{1,0:T(8,128)}, u32[]{:S(2)}) copy-start(f32[15,64]{1,0:T(8,128)} %copy-done.17) | copy-start | bytes 11524
  64.6 4.2 %copy-start.15 = (f32[31,64]{1,0:T(8,128)S(1)}, f32[31,64]{1,0:T(8,128)}, u32[]{:S(2)}) copy-start(f32[31,64]{1,0:T(8,128)} %copy-done.14) | copy-start | bytes 23812
  69.8 6.3 %copy-start.2 = (f32[127,64]{1,0:T(8,128)S(1)}, f32[127,64]{1,0:T(8,128)}, u32[]{:S(2)}) copy-start(f32[127,64]{1,0:T(8,128)} %copy-done.1) | copy-start | bytes 97540
  70.8 6.6 %copy-start.24 = (f32[1,12,64]{2,0,1:T(1,128)S(1)}, f32[1,12,64]{2,0,1:T(1,128)}, u32[]{:S(2)}) copy-start(f32[1,12,64]{2,0,1:T(1,128)} %slice.1781) | copy-start | bytes 9220
  77.4 6.8 %copy-start.3 = (f32[256,64]{1,0:T(8,128)S(1)}, f32[256,64]{1,0:T(8,128)}, u32[]{:S(2)}) copy-start(f32[256,64]{1,0:T(8,128)} %add.305) | copy-start | bytes 196612
  77.4 6.8 %copy-start.32 = (f32[12,64]{1,0:T(8,128)S(1)}, f32[12,64]{1,0:T(8,128)}, u32[]{:S(2)}) copy-start(f32[12,64]{1,0:T(8,128)} %param.8) | copy-start | bytes 9220
  85.6 2.2 copy-start.29
  87.8 2.1 copy-start.9
  176.2 1.9 copy-start.11
  221.1 1.9 copy-start.12
  274.5 40.8 %all-to-all-start.1 = ((f32[18,8,2048]{2,0,1:T(8,128)}), f32[18,8,2048]{2,0,1:T(8,128)S(1)}, u32[]{:S(2)}, u32[]{:S(2)}) async-start(f32[18,8,2048]{2,0,1:T(8,128)} %copy.67), calls=%async_computation.1 | async-start | bytes 3145728 | tf_op jit(solution)/shard_map/all_to_all | solution.py:125
  315.3 10.5 %all-to-all-start.2 = ((f32[1,8,2048]{2,0,1:T(1,128)}), f32[1,8,2048]{2,0,1:T(1,128)S(1)}, u32[]{:S(2)}, u32[]{:S(2)}) async-start(f32[1,8,2048]{2,0,1:T(1,128)} %bitcast.332), calls=%async_computation.2 | async-start | bytes 131072 | tf_op jit(solution)/shard_map/all_to_all | solution.py:132
  319.0 87.9 %all-reduce.35.cloned.1.call-start = ((), (), s32[]{:S(2)}) async-start(), calls=%async_computation.3 | async-start | bytes 6553600 | tf_op jit(solution)/shard_map/psum | solution.py:150
  320.0 5.9 %copy-start.22 = (s32[128,128]{1,0:T(8,128)S(1)}, s32[128,128]{1,0:T(8,128)}, u32[]{:S(2)}) copy-start(s32[128,128]{1,0:T(8,128)} %copy-done.21) | copy-start | bytes 196612
  (7 other events, 5.3 us)
Sparse Core Ops, SparseCore 0:
  338.6 68.2 all-reduce.34
where the time goes:
time: 424 us; the launch traced here: 417 us
  waiting for transfers between devices  129 us (30%)
  other arithmetic  119 us (28%)
  matrix products  81.8 us (19%)
  local copies, waits for them, and re-layouts  56.4 us (13%)
  between operations  15.3 us (4%)
  starting transfers between devices  15.2 us (4%)
    psum x1, waiting for transfers between devices, body(): full_sums, full_counts = lax.psum((cell_sums, cell_counts), 'group')  68.4 us
    mul x4, other arithmetic, solve_spd(): middle.append(total * inverse[outer])  55.1 us
    dot_general x4, matrix products, speciate(): jnp.einsum('pi,pj,pn->ijn', stoich, stoich, complexes, precision=lax.Prec...  51.5 us
    all_to_all x1, waiting for transfers between devices, body(): lax.all_to_all(slot_sums.reshape(width, flow_count, capacity), 'flow', sp...  35.2 us
    mul x4, other arithmetic, solve_spd(): result[outer] = total * inverse[outer]  26.1 us
    all_to_all x1, waiting for transfers between devices, body(): lax.all_to_all(outgoing.reshape(count_comp, flow_count, capacity), 'flow'...  20.7 us
    mul x4, other arithmetic, solve_spd(): lower[outer, inner] = total * inverse[inner]  16.8 us
    another operation x4, local copies, waits for them, and re-layouts, speciate(): logfree = logfree + jnp.stack(update)  14.8 us
  transfers between devices with their start and end apart: 4, of which 4 were waited for; matrix products, arithmetic and copies ran while one was open for 2% of the time, Pallas kernels for 0%

commit v1 on v0

v1 whole, which is shorter than its diff:
```python
import functools

import jax
import jax.numpy as jnp
from jax import lax
from jax.experimental import pallas as pl
from jax.experimental.pallas import tpu as pltpu
from jax.sharding import PartitionSpec as P

ITERS = 4
WIN = 128
LIMIT = 56 * 1024 * 1024
MESH = pl.DeviceIdType.MESH


def blend(factors, values):
    total = factors[0] * values[0]
    for factor, value in zip(factors[1:], values[1:]):
        total = total + factor * value
    return total


def factor_and_solve(matrix, rhs):
    order = len(rhs)
    lower, inverse, middle = {}, [], []
    for p in range(order):
        for r in range(p + 1):
            total = matrix(p, r)
            for o in range(r):
                total = total - lower[p, o] * lower[r, o]
            if p == r:
                inverse.append(lax.rsqrt(total))
            else:
                lower[p, r] = total * inverse[r]
        total = rhs[p]
        for o in range(p):
            total = total - lower[p, o] * middle[o]
        middle.append(total * inverse[p])
    value = [None] * order
    for p in reversed(range(order)):
        total = middle[p]
        for o in range(p + 1, order):
            total = total - lower[o, p] * value[o]
        value[p] = total * inverse[p]
    return value


def newton(totals, stoich, pairs, logk):
    comps, plexes = len(totals), len(logk)
    columns = [[stoich[p][c] for p in range(plexes)] for c in range(comps)]
    logfree = [jnp.log(t) for t in totals]
    over = [1.0 / t for t in totals]
    backs = [jnp.exp(-(logk[p] + blend(stoich[p], logfree))) for p in range(plexes)]

    def small(p, r):
        total = blend(pairs[p, r], over)
        return total + backs[p] if p == r else total

    value = factor_and_solve(small, [jnp.ones_like(totals[0])] * plexes)
    logfree = [x - o * blend(s, value) for x, o, s in zip(logfree, over, columns)]
    for sweep in range(1, ITERS):
        free = [jnp.exp(x) for x in logfree]
        roots = [jnp.exp(0.5 * (logk[p] + blend(stoich[p], logfree))) for p in range(plexes)]
        mixed = [[s[p] * roots[p] for p in range(plexes)] for s in columns]
        rhs = [f + blend(m, roots) - t for f, m, t in zip(free, mixed, totals)]

        def full(p, r):
            total = blend(mixed[p], mixed[r])
            return total + free[p] if p == r else total

        update = factor_and_solve(full, rhs)
        logfree = [x - u for x, u in zip(logfree, update)]
    plex = [jnp.exp(logk[p] + blend(stoich[p], logfree)) for p in range(plexes)]
    return [jnp.exp(x) for x in logfree] + plex


def forward_kernel(
    sizes,
    stoich_ref,
    state_ref,
    pick_ref,
    slot_ref,
    courant_ref,
    cells_ref,
    picks_ref,
    slots_ref,
    weight_ref,
    scale_ref,
    pairs_ref,
    table_ref,
    turned_ref,
    index_ref,
    own_sem,
    send_sem,
    recv_sem,
    pick_send,
    pick_recv,
):
    flow_count, group_count, parts, members, capacity = sizes
    flow, group = lax.axis_index("flow"), lax.axis_index("group")
    part, rank = lax.rem(group, parts), lax.div(group, parts)
    records = flow_count * capacity
    piece = capacity // members
    others = [
        (flow, lax.rem(rank + m, members) * parts + part) for m in range(1, members)
    ]
    peers = [(lax.rem(flow + d, flow_count), group) for d in range(1, flow_count)]
    barrier = pltpu.get_barrier_semaphore()
    for peer in others + peers:
        pl.semaphore_signal(barrier, inc=1, device_id=peer, device_id_type=MESH)
    per = capacity // WIN
    for k in range(per):
        table_ref[pl.ds(k, flow_count, stride=per), :] = pick_ref[:, k * WIN : (k + 1) * WIN]
    pl.semaphore_wait(barrier, len(others) + len(peers))

    def cut(start, size):
        return pl.ds(pl.multiple_of(start, WIN), size)

    def rows(index):
        return pl.ds(pl.multiple_of(index * per, per), per)

    first = part * records
    for d in range(1, flow_count):
        peer = peers[d - 1]
        pltpu.make_async_remote_copy(
            src_ref=state_ref.at[:, cut(first + peer[0] * capacity + rank * piece, piece)],
            dst_ref=cells_ref.at[:, cut(flow * capacity + rank * piece, piece)],
            send_sem=send_sem.at[0, d],
            recv_sem=recv_sem.at[0, d],
            device_id=peer,
            device_id_type=MESH,
        ).start()
    for d in range(1, flow_count):
        peer = peers[d - 1]
        pltpu.make_async_remote_copy(
            src_ref=table_ref.at[rows(peer[0])],
            dst_ref=picks_ref.at[rows(flow)],
            send_sem=pick_send.at[d],
            recv_sem=pick_recv.at[d],
            device_id=peer,
            device_id_type=MESH,
        ).start()
    mine = [
        pltpu.make_async_copy(
            state_ref.at[:, cut(first + flow * capacity, capacity)],
            cells_ref.at[:, cut(flow * capacity, capacity)],
            own_sem.at[0],
        ),
        pltpu.make_async_copy(table_ref.at[rows(flow)], picks_ref.at[rows(flow)], own_sem.at[1]),
    ]
    for copy in mine:
        copy.start()

    plexes, comps = stoich_ref.shape
    for p in range(plexes):
        for r in range(p + 1):
            for c in range(comps):
                pairs_ref[(p * plexes + r) * comps + c] = stoich_ref[p, c] * stoich_ref[r, c]
    tiles = records // WIN
    left = lax.broadcasted_iota(jnp.int32, (tiles, WIN), 1) < WIN // 2

    def by_tile(ref, view):
        value = ref[...]
        view[...] = jnp.transpose(jnp.concatenate([value, value], axis=0))
        even = view[pl.ds(0, tiles, stride=2), :]
        odd = view[pl.ds(1, tiles, stride=2), :]
        return jnp.where(left, even, odd)

    courant = by_tile(courant_ref, turned_ref)
    scale = 1.0 / (1.0 + courant)
    scale_ref[...] = scale
    weight_ref[...] = courant * scale
    slots_ref[...] = by_tile(slot_ref, index_ref) & (WIN - 1)

    def arrival(d, m):
        source = lax.rem(flow + flow_count - d, flow_count)
        owner = lax.rem(rank + members - m, members)
        span = cut(source * capacity + owner * piece, piece)
        return pltpu.make_async_remote_copy(
            src_ref=cells_ref.at[:, span],
            dst_ref=cells_ref.at[:, span],
            send_sem=send_sem.at[m, d],
            recv_sem=recv_sem.at[m, d],
            device_id=others[m - 1] if m else peers[d - 1],
            device_id_type=MESH,
        )

    for d in range(1, flow_count):
        arrival(d, 0).wait_recv()
        source = lax.rem(flow + flow_count - d, flow_count)
        span = cut(source * capacity + rank * piece, piece)
        for m in range(1, members):
            pltpu.make_async_remote_copy(
                src_ref=cells_ref.at[:, span],
                dst_ref=cells_ref.at[:, span],
                send_sem=send_sem.at[m, d],
                recv_sem=recv_sem.at[m, d],
                device_id=others[m - 1],
                device_id_type=MESH,
            ).start()
    for copy in mine:
        copy.wait()
    for d in range(1, flow_count):
        source = lax.rem(flow + flow_count - d, flow_count)
        pltpu.make_async_remote_copy(
            src_ref=table_ref.at[rows(peers[d - 1][0])],
            dst_ref=picks_ref.at[rows(source)],
            send_sem=pick_send.at[d],
            recv_sem=pick_recv.at[d],
            device_id=peers[d - 1],
            device_id_type=MESH,
        ).wait()
        arrival(d, 0).wait_send()
        for m in range(1, members):
            arrival(d, m).wait()


def forward(stoich, state, pick, slot, courant, sizes):
    flow_count, group_count, parts, members, capacity = sizes
    plexes, comps = stoich.shape
    records = flow_count * capacity
    tiles = records // WIN
    anywhere = pl.BlockSpec(memory_space=pl.ANY)
    vmem = pl.BlockSpec(memory_space=pltpu.VMEM)
    smem = pl.BlockSpec(memory_space=pltpu.SMEM)
    table = jax.ShapeDtypeStruct((tiles, WIN), jnp.float32)
    whole = jax.ShapeDtypeStruct((tiles, WIN), jnp.int32)
    return pl.pallas_call(
        functools.partial(forward_kernel, sizes),
        out_shape=(
            jax.ShapeDtypeStruct((comps, records), jnp.float32),
            whole,
            whole,
            table,
            table,
            jax.ShapeDtypeStruct((plexes * plexes * comps,), jnp.float32),
        ),
        in_specs=[smem, anywhere, vmem, vmem, vmem],
        out_specs=(vmem, vmem, vmem, vmem, vmem, smem),
        scratch_shapes=[
            pltpu.VMEM((tiles, WIN), jnp.int32),
            pltpu.VMEM((2 * tiles, WIN), jnp.float32),
            pltpu.VMEM((2 * tiles, WIN), jnp.int32),
            pltpu.SemaphoreType.DMA((2,)),
            pltpu.SemaphoreType.DMA((members, flow_count)),
            pltpu.SemaphoreType.DMA((members, flow_count)),
            pltpu.SemaphoreType.DMA((flow_count,)),
            pltpu.SemaphoreType.DMA((flow_count,)),
        ],
        compiler_params=pltpu.CompilerParams(
            collective_id=0, has_side_effects=True, vmem_limit_bytes=LIMIT
        ),
    )(stoich, state, pick, slot, courant)


def react_kernel(
    sizes,
    stoich_ref,
    pairs_ref,
    logk_ref,
    cells_ref,
    pick_ref,
    slot_ref,
    weight_ref,
    scale_ref,
    inflow_ref,
    out_ref,
    where_ref,
    moved_ref,
    species_ref,
    sums_ref,
    pair_ref,
    own_sem,
    pair_send,
    pair_recv,
    send_sem,
    recv_sem,
):
    flow_count, group_count, parts, members, capacity = sizes
    comps = cells_ref.shape[0]
    plexes = logk_ref.shape[0]
    width = comps + plexes
    tall = species_ref.shape[0] // (capacity // WIN)
    tiles = pick_ref.shape[0]
    per = capacity // WIN
    half = WIN // 2
    deep = moved_ref.shape[0] // tiles

    flow, group = lax.axis_index("flow"), lax.axis_index("group")
    part, rank = lax.rem(group, parts), lax.div(group, parts)
    share = flow_count * parts // group_count

    def chief_of(which):
        return which * members // parts

    chief = chief_of(part)
    spot = lax.rem(rank + members - chief, members)
    target = part * members + lax.div(flow, share)
    sender = lax.div(group, members)
    sender_group = chief_of(sender) * parts + sender
    sender_flow = lax.rem(group, members) * share
    place = lax.rem(flow, share)

    def column(s):
        return lax.rem(flow + 1 + s, flow_count)

    def to_chief(s, index):
        return pltpu.make_async_remote_copy(
            src_ref=sums_ref.at[column(s)],
            dst_ref=pair_ref.at[index, column(s)],
            send_sem=pair_send.at[s],
            recv_sem=pair_recv.at[index, s],
            device_id=(flow, chief * parts + part),
            device_id_type=MESH,
        )

    def to_owner(s, spot_there):
        return pltpu.make_async_remote_copy(
            src_ref=pair_ref.at[0, column(s)],
            dst_ref=out_ref.at[spot_there],
            send_sem=send_sem.at[s],
            recv_sem=recv_sem.at[spot_there],
            device_id=(column(s), target),
            device_id_type=MESH,
        )

    barrier = pltpu.get_barrier_semaphore()
    for k in range(share):
        source = sender_flow + k

        @pl.when(jnp.logical_or(source != flow, sender_group != group))
        def _():
            pl.semaphore_signal(
                barrier, inc=1, device_id=(source, sender_group), device_id_type=MESH
            )

    @pl.when(spot == 0)
    def _():
        for m in range(1, members):
            pl.semaphore_signal(
                barrier,
                inc=1,
                device_id=(flow, lax.rem(chief + m, members) * parts + part),
                device_id_type=MESH,
            )

    where_ref[...] = jnp.take_along_axis(pick_ref[...] & (WIN - 1), slot_ref[...], axis=1)
    left = lax.broadcasted_iota(jnp.int32, (deep, WIN), 1) < half
    zero = jnp.zeros((deep, WIN), jnp.float32)
    inflow = jnp.concatenate([inflow_ref[...], inflow_ref[...]], axis=1)
    inflow = jnp.concatenate([inflow, zero[comps:]], axis=0)

    def transport(t, carry):
        before_w, before_s, moved = carry
        span = pl.ds(pl.multiple_of(t * WIN, WIN), WIN)
        index = jnp.broadcast_to(where_ref[pl.ds(t, 1), :], (deep, WIN))
        block = jnp.concatenate([cells_ref[:, span], zero[comps:]], axis=0)
        old = jnp.take_along_axis(block, index, axis=1)
        weight = jnp.broadcast_to(weight_ref[pl.ds(t, 1), :], (deep, WIN))
        source = old * jnp.broadcast_to(scale_ref[pl.ds(t, 1), :], (deep, WIN))
        turned_w = pltpu.roll(weight, half, 1)
        turned_s = pltpu.roll(source, half, 1)
        both = weight * jnp.where(left, before_w, turned_w)
        added = weight * jnp.where(left, before_s, turned_s) + source
        moved = both * moved + added
        moved_ref[pl.ds(pl.multiple_of(t * deep, deep), deep), :] = moved
        return turned_w, turned_s, moved

    lax.fori_loop(0, tiles, transport, (zero + 1.0, zero, inflow), unroll=8)

    stoich = [[stoich_ref[p, c] for c in range(comps)] for p in range(plexes)]
    logk = [logk_ref[p] for p in range(plexes)]
    pairs = {}
    for p in range(plexes):
        for r in range(p + 1):
            base = (p * plexes + r) * comps
            pairs[p, r] = [pairs_ref[base + c] for c in range(comps)]
    species_ref[...] = jnp.ones_like(species_ref)
    lanes = lax.broadcasted_iota(jnp.int32, (WIN, WIN), 0)

    def deposit(s):
        for row in range(per):
            value = species_ref[row * tall : (row + 1) * tall, :]
            high = value.astype(jnp.bfloat16).astype(jnp.float32)
            both = jnp.concatenate([high, value - high], axis=0).astype(jnp.bfloat16)
            index = where_ref[pl.ds(column(s) * per + row, 1), :]
            table = jnp.where(lanes == jnp.broadcast_to(index, (WIN, WIN)), 1.0, 0.0)
            sums = lax.dot_general(
                both,
                table.astype(jnp.bfloat16),
                (((1,), (1,)), ((), ())),
                preferred_element_type=jnp.float32,
            )
            total = sums[:tall] + sums[tall:]
            sums_ref[column(s), row * (width + 1) : (row + 1) * (width + 1), :] = total[: width + 1]

    def hand_on(s):
        for index in range(members - 1):

            @pl.when(spot == index + 1)
            def _():
                to_chief(s, index).start()

    def add_up(s):
        for index in range(members - 1):
            to_chief(s, index).wait_recv()
        total = sums_ref[column(s)] + pair_ref[0, column(s)]
        for index in range(1, members - 1):
            total = total + pair_ref[index, column(s)]
        pair_ref[0, column(s)] = total

    def step(s, carry):
        deposit(jnp.maximum(s - 1, 0))
        base = column(s) * (per * deep)
        totals = [moved_ref[pl.ds(base + c, per, stride=deep), :] for c in range(comps)]
        for q, value in enumerate(newton(totals, stoich, pairs, logk)):
            species_ref[pl.ds(q, per, stride=tall), :] = value

        @pl.when(s == 1)
        def _():
            @pl.when(spot != 0)
            def _():
                pl.semaphore_wait(barrier, 1)

            @pl.when(jnp.logical_and(spot == 0, target == group))
            def _():
                pl.semaphore_wait(barrier, flow_count - 1)

            @pl.when(jnp.logical_and(spot == 0, target != group))
            def _():
                pl.semaphore_wait(barrier, flow_count)

        @pl.when(s >= 1)
        def _():
            hand_on(s - 1)

        @pl.when(jnp.logical_and(s >= 2, spot == 0))
        def _():
            add_up(s - 2)
            to_owner(s - 2, place).start()

        return carry

    lax.fori_loop(0, flow_count, step, 0)
    last = flow_count - 1
    deposit(last)
    hand_on(last)

    @pl.when(spot == 0)
    def _():
        add_up(last - 1)
        to_owner(last - 1, place).start()
        add_up(last)

        @pl.when(target != group)
        def _():
            to_owner(last, place).start()
            to_owner(last, place).wait_send()

        @pl.when(target == group)
        def _():
            copy = pltpu.make_async_copy(pair_ref.at[0, flow], out_ref.at[place], own_sem)
            copy.start()
            copy.wait()

        for s in range(last):
            to_owner(s, place).wait_send()

    @pl.when(spot != 0)
    def _():
        for s in range(flow_count):
            to_chief(s, 0).wait_send()

    for k in range(share):
        source = sender_flow + k

        @pl.when(jnp.logical_or(source != flow, sender_group != group))
        def _():
            to_owner(0, k).wait_recv()


def react(cells, pick, slot, weight, scale, inflow, stoich, pairs, logk, sizes):
    flow_count, group_count, parts, members, capacity = sizes
    comps = cells.shape[0]
    tiles = pick.shape[0]
    per = capacity // WIN
    width = comps + logk.shape[0]
    deep = -(-comps // 8) * 8
    tall = -(-(width + 1) // 8) * 8
    share = flow_count * parts // group_count
    smem = pl.BlockSpec(memory_space=pltpu.SMEM)
    vmem = pl.BlockSpec(memory_space=pltpu.VMEM)
    chunk = (per * (width + 1), WIN)
    return pl.pallas_call(
        functools.partial(react_kernel, sizes),
        out_shape=jax.ShapeDtypeStruct((share,) + chunk, jnp.float32),
        in_specs=[smem] * 3 + [vmem] * 6,
        out_specs=vmem,
        scratch_shapes=[
            pltpu.VMEM((tiles, WIN), jnp.int32),
            pltpu.VMEM((tiles * deep, WIN), jnp.float32),
            pltpu.VMEM((per * tall, WIN), jnp.float32),
            pltpu.VMEM((flow_count,) + chunk, jnp.float32),
            pltpu.VMEM((members - 1, flow_count) + chunk, jnp.float32),
            pltpu.SemaphoreType.DMA,
            pltpu.SemaphoreType.DMA((flow_count,)),
            pltpu.SemaphoreType.DMA((members - 1, flow_count)),
            pltpu.SemaphoreType.DMA((flow_count,)),
            pltpu.SemaphoreType.DMA((share,)),
        ],
        compiler_params=pltpu.CompilerParams(
            collective_id=1, has_side_effects=True, vmem_limit_bytes=LIMIT
        ),
    )(stoich, pairs, logk, cells, pick, slot, weight, scale, inflow)


def mean_kernel(sums_ref, out_ref):
    width = out_ref.shape[0]
    tall = width + 1
    share, height = sums_ref.shape[:2]
    per = height // tall
    for k in range(share):
        for row in range(per):
            value = sums_ref[k, row * tall : row * tall + width, :]
            count = sums_ref[k, row * tall + width : (row + 1) * tall, :]
            tile = k * per + row
            out_ref[:, tile * WIN : (tile + 1) * WIN] = value / jnp.maximum(count, 1.0)


def mean(sums, width):
    share, height = sums.shape[:2]
    vmem = pl.BlockSpec(memory_space=pltpu.VMEM)
    return pl.pallas_call(
        mean_kernel,
        out_shape=jax.ShapeDtypeStruct((width, share * height // (width + 1) * WIN), jnp.float32),
        in_specs=[vmem],
        out_specs=vmem,
        compiler_params=pltpu.CompilerParams(vmem_limit_bytes=LIMIT),
    )(sums)


def body(cell_state, inflow, courant, pick, node_slot, stoich, logk):
    cell_count = cell_state.shape[1]
    flow_count, group_count = lax.axis_size("flow"), lax.axis_size("group")
    capacity = pick.shape[3]
    parts = cell_count // (flow_count * capacity)
    sizes = (flow_count, group_count, parts, group_count // parts, capacity)
    cells, picks, slots, weight, scale, pairs = forward(
        stoich, cell_state, pick.reshape(flow_count, capacity), node_slot.T, courant.T, sizes
    )
    sums = react(cells, picks, slots, weight, scale, inflow, stoich, pairs, logk, sizes)
    return mean(sums, cell_state.shape[0] + logk.shape[0])


def solution(mesh):
    placed = (
        P(None, "flow"),
        P(None, ("flow", "group")),
        P(None, ("flow", "group")),
        P("group", "flow", None, None),
        P(None, ("flow", "group")),
        P(),
        P(),
    )
    return jax.shard_map(
        body, mesh=mesh, in_specs=placed, out_specs=P(None, ("flow", "group")), check_vma=False
    )
```

time: 424 us -> 63.8 us (0.15); the launches traced: 417 us -> 63.6 us
  waiting for transfers between devices: 129 us -> 0 us
  other arithmetic: 119 us -> 0 us
  matrix products: 81.8 us -> 0 us
  Pallas kernels: 0 us -> 63.6 us
  local copies, waits for them, and re-layouts: 56.4 us -> 0 us
  between operations: 15.3 us -> 0.02 us
  starting transfers between devices: 15.2 us -> 0 us
    mul x26 -> x0, other arithmetic: 98.8 us -> none  [the longest x4 55.1 us: solve_spd(): middle.append(total * inverse[outer])]
    dot_general x17 -> x0, matrix products: 81.8 us -> none  [the longest x4 51.5 us: speciate(): jnp.einsum('pi,pj,pn->ijn', stoich, stoich, complexes, precision=lax.Prec...]
    psum x1 -> x0, waiting for transfers between devices: 68.4 us -> none  [body(): full_sums, full_counts = lax.psum((cell_sums, cell_counts), 'group')]
    pallas_call x0 -> x3, Pallas kernels: none -> 63.6 us  [the longest x1 35.5 us: react(): pl.pallas_call(functools.partial(react_kernel, sizes), out_shape=jax.Shap...]
    all_to_all x3 -> x0, waiting for transfers between devices: 60.9 us -> none  [the longest x1 35.2 us: body(): lax.all_to_all(slot_sums.reshape(width, flow_count, capacity), 'flow', sp...]
    all_to_all x3 -> x0, starting transfers between devices: 14.9 us -> none  [the longest x1 7.66 us: body(): lax.all_to_all(outgoing.reshape(count_comp, flow_count, capacity), 'flow'...]
    another operation x4 -> x0, local copies, waits for them, and re-layouts: 14.8 us -> none  [speciate(): logfree = logfree + jnp.stack(update)]
    pad x28 -> x0, local copies, waits for them, and re-layouts: 12.6 us -> none  [body(): lax.associative_scan(compose_nodes, (weight, source), axis=0)]
  transfers between devices with their start and end apart: 4 -> 0, of which waited for: 4 -> 0; matrix products, arithmetic and copies ran while one was open for 2% -> 0% of each run, Pallas kernels for 0% -> 0%
where the time goes in v1:
time: 63.8 us; the launch traced here: 63.6 us
  Pallas kernels  63.6 us (100%)
    pallas_call x1, Pallas kernels, react(): pl.pallas_call(functools.partial(react_kernel, sizes), out_shape=jax.Shap...  35.5 us
    pallas_call x1, Pallas kernels, forward(): pl.pallas_call(functools.partial(forward_kernel, sizes), out_shape=(jax.S...  26.1 us
    pallas_call x1, Pallas kernels, mean(): pl.pallas_call(mean_kernel, out_shape=jax.ShapeDtypeStruct((width, share...  2.03 us

profile of v1, /device:TPU:0, one launch (start us, length us, event | category | flops | bytes accessed | tf_op | source)
XLA Modules:
  0.0 63.6 jit_solution(15483344441065400681)
XLA Ops:
  0.0 26.1 %shard_map.73 = (f32[12,16384]{1,0:T(8,128)}, s32[128,128]{1,0:T(8,128)}, s32[128,128]{1,0:T(8,128)}, f32[128,128]{1,0:T(8,128)}, f32[128,128]{1,0:T(8,128)}, /*index=5*/f32[432]{0:T(512)}) custom-call(f32[6,12]{1,0:T(8,128)} %stoich_ref.3, f32[12,32768]{1,0:T(8,128)} %state_ref.1, s32[8,2048]{1,0:T(8,128)} %bitcast.3, s32[64,256]{1,0:T(8,128)} %bitcast.4, ...), custom_call_target="tpu_custom_call" | custom-call | tf_op jit(solution)/shard_map/pallas_call | solution.py:228
  26.1 35.5 %shard_map.74.sums_ref = f32[4,304,128]{2,1,0:T(8,128)} custom-call(f32[6,12]{1,0:T(8,128)} %stoich_ref.3, f32[432]{0:T(512)} %get-tuple-element.11.pairs_ref, f32[6]{0:T(128)} %logk_ref.1, f32[12,16384]{1,0:T(8,128)} %get-tuple-element.12.cells_ref, s32[128,128]{1,0:T(8,128)} %get-tuple-element.13.pick_ref, s32[128,128]{1,0:T(8,128)} %get-tuple-element.14.slot_ref, ...), custom_call_target="tpu_custom_call" | custom-call | tf_op jit(solution)/shard_map/pallas_call | solution.py:494
  61.6 2.0 %shard_map.75 = f32[18,8192]{1,0:T(8,128)} custom-call(f32[4,304,128]{2,1,0:T(8,128)} %shard_map.74.sums_ref), custom_call_target="tpu_custom_call" | custom-call | tf_op jit(solution)/shard_map/pallas_call | solution.py:533

commit v2 on v1

--- a/solution.py
+++ b/solution.py
@@ -2,6 +2,7 @@
 
 import jax
 import jax.numpy as jnp
+import numpy as np
 from jax import lax
 from jax.experimental import pallas as pl
 from jax.experimental.pallas import tpu as pltpu
@@ -45,7 +46,22 @@
     return value
 
 
-def newton(totals, stoich, pairs, logk):
+def entry(p, r):
+    return p * (p + 1) // 2 + r
+
+
+def spread(comps, plexes):
+    first = np.zeros((comps * (comps + 1) // 2 * 8, comps), np.float32)
+    second = np.zeros_like(first)
+    for p in range(comps):
+        for r in range(p + 1):
+            first[entry(p, r) * 8 : entry(p, r) * 8 + 8, p] = 1.0
+            second[entry(p, r) * 8 : entry(p, r) * 8 + 8, r] = 1.0
+    across = np.kron(np.eye(plexes, dtype=np.float32), np.ones((1, 8), np.float32))
+    return first, second, across
+
+
+def newton(totals, stoich, pairs, logk, weights_ref, matrix_ref):
     comps, plexes = len(totals), len(logk)
     columns = [[stoich[p][c] for p in range(plexes)] for c in range(comps)]
     logfree = [jnp.log(t) for t in totals]
@@ -60,12 +76,16 @@
     logfree = [x - o * blend(s, value) for x, o, s in zip(logfree, over, columns)]
     for sweep in range(1, ITERS):
         free = [jnp.exp(x) for x in logfree]
-        roots = [jnp.exp(0.5 * (logk[p] + blend(stoich[p], logfree))) for p in range(plexes)]
-        mixed = [[s[p] * roots[p] for p in range(plexes)] for s in columns]
-        rhs = [f + blend(m, roots) - t for f, m, t in zip(free, mixed, totals)]
+        plex = [jnp.exp(logk[p] + blend(stoich[p], logfree)) for p in range(plexes)]
+        stack = jnp.concatenate(plex, axis=0)
+        high = stack.astype(jnp.bfloat16)
+        low = (stack - high.astype(jnp.float32)).astype(jnp.bfloat16)
+        parts = jnp.concatenate([high, high, high, low, low], axis=0)
+        matrix_ref[...] = jnp.dot(weights_ref[...], parts, preferred_element_type=jnp.float32)
+        rhs = [f + blend(s, plex) - t for f, s, t in zip(free, columns, totals)]
 
         def full(p, r):
-            total = blend(mixed[p], mixed[r])
+            total = matrix_ref[entry(p, r) * 8 : entry(p, r) * 8 + 8, :]
             return total + free[p] if p == r else total
 
         update = factor_and_solve(full, rhs)
@@ -77,6 +97,10 @@
 def forward_kernel(
     sizes,
     stoich_ref,
+    table_s_ref,
+    first_ref,
+    second_ref,
+    across_ref,
     state_ref,
     pick_ref,
     slot_ref,
@@ -87,6 +111,7 @@
     weight_ref,
     scale_ref,
     pairs_ref,
+    weights_ref,
     table_ref,
     turned_ref,
     index_ref,
@@ -156,6 +181,20 @@
         for r in range(p + 1):
             for c in range(comps):
                 pairs_ref[(p * plexes + r) * comps + c] = stoich_ref[p, c] * stoich_ref[r, c]
+    exact = functools.partial(
+        lax.dot_general, precision=lax.Precision.HIGHEST, preferred_element_type=jnp.float32
+    )
+    wide = exact(table_s_ref[...], across_ref[...], (((0,), (0,)), ((), ())))
+    products = exact(first_ref[...], wide, (((1,), (0,)), ((), ())))
+    products = products * exact(second_ref[...], wide, (((1,), (0,)), ((), ())))
+    place = [lax.rem(lax.broadcasted_iota(jnp.int32, products.shape, k), 8) for k in range(2)]
+    products = jnp.where(place[0] == place[1], products, 0.0)
+    high = products.astype(jnp.bfloat16).astype(jnp.float32)
+    rest = products - high
+    middle = rest.astype(jnp.bfloat16).astype(jnp.float32)
+    split = jnp.concatenate([high, middle, rest - middle, high, middle], axis=1)
+    weights_ref[...] = split.astype(jnp.bfloat16)
+
     tiles = records // WIN
     left = lax.broadcasted_iota(jnp.int32, (tiles, WIN), 1) < WIN // 2
 
@@ -218,6 +257,7 @@
 def forward(stoich, state, pick, slot, courant, sizes):
     flow_count, group_count, parts, members, capacity = sizes
     plexes, comps = stoich.shape
+    first, second, across = spread(comps, plexes)
     records = flow_count * capacity
     tiles = records // WIN
     anywhere = pl.BlockSpec(memory_space=pl.ANY)
@@ -234,9 +274,10 @@
             table,
             table,
             jax.ShapeDtypeStruct((plexes * plexes * comps,), jnp.float32),
+            jax.ShapeDtypeStruct((first.shape[0], 5 * 8 * plexes), jnp.bfloat16),
         ),
-        in_specs=[smem, anywhere, vmem, vmem, vmem],
-        out_specs=(vmem, vmem, vmem, vmem, vmem, smem),
+        in_specs=[smem, vmem, vmem, vmem, vmem, anywhere, vmem, vmem, vmem],
+        out_specs=(vmem, vmem, vmem, vmem, vmem, smem, vmem),
         scratch_shapes=[
             pltpu.VMEM((tiles, WIN), jnp.int32),
             pltpu.VMEM((2 * tiles, WIN), jnp.float32),
@@ -250,7 +291,7 @@
         compiler_params=pltpu.CompilerParams(
             collective_id=0, has_side_effects=True, vmem_limit_bytes=LIMIT
         ),
-    )(stoich, state, pick, slot, courant)
+    )(stoich, stoich, first, second, across, state, pick, slot, courant)
 
 
 def react_kernel(
@@ -264,8 +305,10 @@
     weight_ref,
     scale_ref,
     inflow_ref,
+    weights_ref,
     out_ref,
     where_ref,
+    matrix_ref,
     moved_ref,
     species_ref,
     sums_ref,
@@ -412,9 +455,19 @@
     def step(s, carry):
         deposit(jnp.maximum(s - 1, 0))
         base = column(s) * (per * deep)
-        totals = [moved_ref[pl.ds(base + c, per, stride=deep), :] for c in range(comps)]
-        for q, value in enumerate(newton(totals, stoich, pairs, logk)):
-            species_ref[pl.ds(q, per, stride=tall), :] = value
+        totals = []
+        for c in range(comps):
+            blocks = [
+                moved_ref[pl.ds(base + 8 * k * deep + c, 8, stride=deep), :]
+                for k in range(per // 8)
+            ]
+            totals.append(jnp.concatenate(blocks, axis=1))
+        species = newton(totals, stoich, pairs, logk, weights_ref, matrix_ref)
+        for q, value in enumerate(species):
+            for k in range(per // 8):
+                species_ref[pl.ds(8 * k * tall + q, 8, stride=tall), :] = value[
+                    :, k * WIN : (k + 1) * WIN
+                ]
 
         @pl.when(s == 1)
         def _():
@@ -479,7 +532,7 @@
             to_owner(0, k).wait_recv()
 
 
-def react(cells, pick, slot, weight, scale, inflow, stoich, pairs, logk, sizes):
+def react(cells, pick, slot, weight, scale, inflow, weights, stoich, pairs, logk, sizes):
     flow_count, group_count, parts, members, capacity = sizes
     comps = cells.shape[0]
     tiles = pick.shape[0]
@@ -494,10 +547,11 @@
     return pl.pallas_call(
         functools.partial(react_kernel, sizes),
         out_shape=jax.ShapeDtypeStruct((share,) + chunk, jnp.float32),
-        in_specs=[smem] * 3 + [vmem] * 6,
+        in_specs=[smem] * 3 + [vmem] * 7,
         out_specs=vmem,
         scratch_shapes=[
             pltpu.VMEM((tiles, WIN), jnp.int32),
+            pltpu.VMEM((weights.shape[0], per * WIN // 8), jnp.float32),
             pltpu.VMEM((tiles * deep, WIN), jnp.float32),
             pltpu.VMEM((per * tall, WIN), jnp.float32),
             pltpu.VMEM((flow_count,) + chunk, jnp.float32),
@@ -511,30 +565,27 @@
         compiler_params=pltpu.CompilerParams(
             collective_id=1, has_side_effects=True, vmem_limit_bytes=LIMIT
         ),
-    )(stoich, pairs, logk, cells, pick, slot, weight, scale, inflow)
+    )(stoich, pairs, logk, cells, pick, slot, weight, scale, inflow, weights)
 
 
 def mean_kernel(sums_ref, out_ref):
     width = out_ref.shape[0]
     tall = width + 1
-    share, height = sums_ref.shape[:2]
-    per = height // tall
-    for k in range(share):
-        for row in range(per):
-            value = sums_ref[k, row * tall : row * tall + width, :]
-            count = sums_ref[k, row * tall + width : (row + 1) * tall, :]
-            tile = k * per + row
-            out_ref[:, tile * WIN : (tile + 1) * WIN] = value / jnp.maximum(count, 1.0)
+    for row in range(sums_ref.shape[1] // tall):
+        value = sums_ref[0, row * tall : row * tall + width, :]
+        count = sums_ref[0, row * tall + width : (row + 1) * tall, :]
+        out_ref[:, row * WIN : (row + 1) * WIN] = value / jnp.maximum(count, 1.0)
 
 
 def mean(sums, width):
     share, height = sums.shape[:2]
-    vmem = pl.BlockSpec(memory_space=pltpu.VMEM)
+    columns = height // (width + 1) * WIN
     return pl.pallas_call(
         mean_kernel,
-        out_shape=jax.ShapeDtypeStruct((width, share * height // (width + 1) * WIN), jnp.float32),
-        in_specs=[vmem],
-        out_specs=vmem,
+        out_shape=jax.ShapeDtypeStruct((width, share * columns), jnp.float32),
+        grid=(share,),
+        in_specs=[pl.BlockSpec((1, height, WIN), lambda k: (k, 0, 0))],
+        out_specs=pl.BlockSpec((width, columns), lambda k: (0, k)),
         compiler_params=pltpu.CompilerParams(vmem_limit_bytes=LIMIT),
     )(sums)
 
@@ -545,10 +596,10 @@
     capacity = pick.shape[3]
     parts = cell_count // (flow_count * capacity)
     sizes = (flow_count, group_count, parts, group_count // parts, capacity)
-    cells, picks, slots, weight, scale, pairs = forward(
+    cells, picks, slots, weight, scale, pairs, weights = forward(
         stoich, cell_state, pick.reshape(flow_count, capacity), node_slot.T, courant.T, sizes
     )
-    sums = react(cells, picks, slots, weight, scale, inflow, stoich, pairs, logk, sizes)
+    sums = react(cells, picks, slots, weight, scale, inflow, weights, stoich, pairs, logk, sizes)
     return mean(sums, cell_state.shape[0] + logk.shape[0])
 
 

time: 63.8 us -> 62 us (0.972)
  Pallas kernels: 63.6 us -> 61.2 us
    pallas_call x1, Pallas kernels: 35.5 us -> 31.5 us  [react(): pl.pallas_call(functools.partial(react_kernel, sizes), out_shape=jax.Shap...]
    pallas_call x1, Pallas kernels: 2.03 us -> 3.25 us  [mean(): pl.pallas_call(mean_kernel, out_shape=jax.ShapeDtypeStruct((width, share...]
where the time goes in v2:
time: 62 us; the launch traced here: 61.2 us
  Pallas kernels  61.2 us (99%)
    pallas_call x1, Pallas kernels, react(): pl.pallas_call(functools.partial(react_kernel, sizes), out_shape=jax.Shap...  31.5 us
    pallas_call x1, Pallas kernels, forward(): pl.pallas_call(functools.partial(forward_kernel, sizes), out_shape=(jax.S...  26.4 us
    pallas_call x1, Pallas kernels, mean(): pl.pallas_call(mean_kernel, out_shape=jax.ShapeDtypeStruct((width, share...  3.25 us

profile of v2, /device:TPU:0, one launch (start us, length us, event | category | flops | bytes accessed | tf_op | source)
XLA Modules:
  0.0 61.2 jit_solution(11906306072700798868)
XLA Ops:
  0.0 26.4 %shard_map.100 = (f32[12,16384]{1,0:T(8,128)}, s32[128,128]{1,0:T(8,128)}, s32[128,128]{1,0:T(8,128)}, f32[128,128]{1,0:T(8,128)}, f32[128,128]{1,0:T(8,128)}, /*index=5*/f32[432]{0:T(512)}, bf16[624,240]{1,0:T(8,128)(2,1)}) custom-call(f32[6,12]{1,0:T(8,128)} %stoich_ref.3, f32[6,12]{1,0:T(8,128)} %stoich_ref.3, f32[624,12]{1,0:T(8,128)} %constant.6.clone.first_ref, ...), custom_call_target="tpu_custom_call" | custom-call | tf_op jit(solution)/shard_map/pallas_call | solution.py:268
  26.4 31.5 %shard_map.101.sums_ref = f32[4,304,128]{2,1,0:T(8,128)} custom-call(f32[6,12]{1,0:T(8,128)} %stoich_ref.3, f32[432]{0:T(512)} %get-tuple-element.12.pairs_ref, f32[6]{0:T(128)} %logk_ref.1, f32[12,16384]{1,0:T(8,128)} %get-tuple-element.13.cells_ref, s32[128,128]{1,0:T(8,128)} %get-tuple-element.14.pick_ref, s32[128,128]{1,0:T(8,128)} %get-tuple-element.15.slot_ref, ...), custom_call_target="tpu_custom_call" | custom-call | tf_op jit(solution)/shard_map/pallas_call | solution.py:547
  57.9 3.2 %shard_map.102 = f32[18,8192]{1,0:T(8,128)} custom-call(f32[4,304,128]{2,1,0:T(8,128)} %shard_map.101.sums_ref), custom_call_target="tpu_custom_call" | custom-call | tf_op jit(solution)/shard_map/pallas_call | solution.py:583

commit v3 on v2

--- a/solution.py
+++ b/solution.py
@@ -454,6 +454,25 @@
 
     def step(s, carry):
         deposit(jnp.maximum(s - 1, 0))
+
+        @pl.when(s == 1)
+        def _():
+            @pl.when(spot != 0)
+            def _():
+                pl.semaphore_wait(barrier, 1)
+
+            @pl.when(jnp.logical_and(spot == 0, target == group))
+            def _():
+                pl.semaphore_wait(barrier, flow_count - 1)
+
+            @pl.when(jnp.logical_and(spot == 0, target != group))
+            def _():
+                pl.semaphore_wait(barrier, flow_count)
+
+        @pl.when(s >= 1)
+        def _():
+            hand_on(s - 1)
+
         base = column(s) * (per * deep)
         totals = []
         for c in range(comps):
@@ -469,28 +488,10 @@
                     :, k * WIN : (k + 1) * WIN
                 ]
 
-        @pl.when(s == 1)
+        @pl.when(jnp.logical_and(s >= 1, spot == 0))
         def _():
-            @pl.when(spot != 0)
-            def _():
-                pl.semaphore_wait(barrier, 1)
-
-            @pl.when(jnp.logical_and(spot == 0, target == group))
-            def _():
-                pl.semaphore_wait(barrier, flow_count - 1)
-
-            @pl.when(jnp.logical_and(spot == 0, target != group))
-            def _():
-                pl.semaphore_wait(barrier, flow_count)
-
-        @pl.when(s >= 1)
-        def _():
-            hand_on(s - 1)
-
-        @pl.when(jnp.logical_and(s >= 2, spot == 0))
-        def _():
-            add_up(s - 2)
-            to_owner(s - 2, place).start()
+            add_up(s - 1)
+            to_owner(s - 1, place).start()
 
         return carry
 
@@ -501,8 +502,6 @@
 
     @pl.when(spot == 0)
     def _():
-        add_up(last - 1)
-        to_owner(last - 1, place).start()
         add_up(last)
 
         @pl.when(target != group)
@@ -571,21 +570,24 @@
 def mean_kernel(sums_ref, out_ref):
     width = out_ref.shape[0]
     tall = width + 1
-    for row in range(sums_ref.shape[1] // tall):
-        value = sums_ref[0, row * tall : row * tall + width, :]
-        count = sums_ref[0, row * tall + width : (row + 1) * tall, :]
-        out_ref[:, row * WIN : (row + 1) * WIN] = value / jnp.maximum(count, 1.0)
+    share, height = sums_ref.shape[:2]
+    per = height // tall
+    for k in range(share):
+        for row in range(per):
+            value = sums_ref[k, row * tall : row * tall + width, :]
+            count = sums_ref[k, row * tall + width : (row + 1) * tall, :]
+            tile = k * per + row
+            out_ref[:, tile * WIN : (tile + 1) * WIN] = value * (1.0 / jnp.maximum(count, 1.0))
 
 
 def mean(sums, width):
     share, height = sums.shape[:2]
-    columns = height // (width + 1) * WIN
+    vmem = pl.BlockSpec(memory_space=pltpu.VMEM)
     return pl.pallas_call(
         mean_kernel,
-        out_shape=jax.ShapeDtypeStruct((width, share * columns), jnp.float32),
-        grid=(share,),
-        in_specs=[pl.BlockSpec((1, height, WIN), lambda k: (k, 0, 0))],
-        out_specs=pl.BlockSpec((width, columns), lambda k: (0, k)),
+        out_shape=jax.ShapeDtypeStruct((width, share * height // (width + 1) * WIN), jnp.float32),
+        in_specs=[vmem],
+        out_specs=vmem,
         compiler_params=pltpu.CompilerParams(vmem_limit_bytes=LIMIT),
     )(sums)
 

time: 62 us -> 60.6 us (0.977); the launches traced: 61.2 us -> 60.4 us
  Pallas kernels: 61.2 us -> 60.4 us
    pallas_call x1, Pallas kernels: 3.25 us -> 2.03 us  [mean(): pl.pallas_call(mean_kernel, out_shape=jax.ShapeDtypeStruct((width, share...]
where the time goes in v3:
time: 60.6 us; the launch traced here: 60.4 us
  Pallas kernels  60.4 us (100%)
    pallas_call x1, Pallas kernels, react(): pl.pallas_call(functools.partial(react_kernel, sizes), out_shape=jax.Shap...  32 us
    pallas_call x1, Pallas kernels, forward(): pl.pallas_call(functools.partial(forward_kernel, sizes), out_shape=(jax.S...  26.4 us
    pallas_call x1, Pallas kernels, mean(): pl.pallas_call(mean_kernel, out_shape=jax.ShapeDtypeStruct((width, share...  2.03 us

profile of v3, /device:TPU:0, one launch (start us, length us, event | category | flops | bytes accessed | tf_op | source)
XLA Modules:
  0.0 60.4 jit_solution(14311628154770562186)
XLA Ops:
  0.0 26.4 %shard_map.100 = (f32[12,16384]{1,0:T(8,128)}, s32[128,128]{1,0:T(8,128)}, s32[128,128]{1,0:T(8,128)}, f32[128,128]{1,0:T(8,128)}, f32[128,128]{1,0:T(8,128)}, /*index=5*/f32[432]{0:T(512)}, bf16[624,240]{1,0:T(8,128)(2,1)}) custom-call(f32[6,12]{1,0:T(8,128)} %stoich_ref.3, f32[6,12]{1,0:T(8,128)} %stoich_ref.3, f32[624,12]{1,0:T(8,128)} %constant.6.clone.first_ref, ...), custom_call_target="tpu_custom_call" | custom-call | tf_op jit(solution)/shard_map/pallas_call | solution.py:268
  26.4 32.0 %shard_map.101.sums_ref = f32[4,304,128]{2,1,0:T(8,128)} custom-call(f32[6,12]{1,0:T(8,128)} %stoich_ref.3, f32[432]{0:T(512)} %get-tuple-element.12.pairs_ref, f32[6]{0:T(128)} %logk_ref.1, f32[12,16384]{1,0:T(8,128)} %get-tuple-element.13.cells_ref, s32[128,128]{1,0:T(8,128)} %get-tuple-element.14.pick_ref, s32[128,128]{1,0:T(8,128)} %get-tuple-element.15.slot_ref, ...), custom_call_target="tpu_custom_call" | custom-call | tf_op jit(solution)/shard_map/pallas_call | solution.py:546
  58.4 2.0 %shard_map.102 = f32[18,8192]{1,0:T(8,128)} custom-call(f32[4,304,128]{2,1,0:T(8,128)} %shard_map.101.sums_ref), custom_call_target="tpu_custom_call" | custom-call | tf_op jit(solution)/shard_map/pallas_call | solution.py:586

commit v4 on v3

--- a/solution.py
+++ b/solution.py
@@ -177,39 +177,46 @@
         copy.start()
 
     plexes, comps = stoich_ref.shape
-    for p in range(plexes):
-        for r in range(p + 1):
-            for c in range(comps):
-                pairs_ref[(p * plexes + r) * comps + c] = stoich_ref[p, c] * stoich_ref[r, c]
-    exact = functools.partial(
-        lax.dot_general, precision=lax.Precision.HIGHEST, preferred_element_type=jnp.float32
-    )
-    wide = exact(table_s_ref[...], across_ref[...], (((0,), (0,)), ((), ())))
-    products = exact(first_ref[...], wide, (((1,), (0,)), ((), ())))
-    products = products * exact(second_ref[...], wide, (((1,), (0,)), ((), ())))
-    place = [lax.rem(lax.broadcasted_iota(jnp.int32, products.shape, k), 8) for k in range(2)]
-    products = jnp.where(place[0] == place[1], products, 0.0)
-    high = products.astype(jnp.bfloat16).astype(jnp.float32)
-    rest = products - high
-    middle = rest.astype(jnp.bfloat16).astype(jnp.float32)
-    split = jnp.concatenate([high, middle, rest - middle, high, middle], axis=1)
-    weights_ref[...] = split.astype(jnp.bfloat16)
-
-    tiles = records // WIN
-    left = lax.broadcasted_iota(jnp.int32, (tiles, WIN), 1) < WIN // 2
-
-    def by_tile(ref, view):
-        value = ref[...]
-        view[...] = jnp.transpose(jnp.concatenate([value, value], axis=0))
-        even = view[pl.ds(0, tiles, stride=2), :]
-        odd = view[pl.ds(1, tiles, stride=2), :]
-        return jnp.where(left, even, odd)
-
-    courant = by_tile(courant_ref, turned_ref)
-    scale = 1.0 / (1.0 + courant)
-    scale_ref[...] = scale
-    weight_ref[...] = courant * scale
-    slots_ref[...] = by_tile(slot_ref, index_ref) & (WIN - 1)
+
+    def scalar_products():
+        for p in range(plexes):
+            for r in range(p + 1):
+                for c in range(comps):
+                    pairs_ref[(p * plexes + r) * comps + c] = stoich_ref[p, c] * stoich_ref[r, c]
+
+    def entry_weights():
+        exact = functools.partial(
+            lax.dot_general, precision=lax.Precision.HIGHEST, preferred_element_type=jnp.float32
+        )
+        wide = exact(table_s_ref[...], across_ref[...], (((0,), (0,)), ((), ())))
+        products = exact(first_ref[...], wide, (((1,), (0,)), ((), ())))
+        products = products * exact(second_ref[...], wide, (((1,), (0,)), ((), ())))
+        place = [lax.rem(lax.broadcasted_iota(jnp.int32, products.shape, k), 8) for k in range(2)]
+        products = jnp.where(place[0] == place[1], products, 0.0)
+        high = products.astype(jnp.bfloat16).astype(jnp.float32)
+        rest = products - high
+        middle = rest.astype(jnp.bfloat16).astype(jnp.float32)
+        split = jnp.concatenate([high, middle, rest - middle, high, middle], axis=1)
+        weights_ref[...] = split.astype(jnp.bfloat16)
+
+    def transport_weights():
+        tiles = records // WIN
+        left = lax.broadcasted_iota(jnp.int32, (tiles, WIN), 1) < WIN // 2
+
+        def by_tile(ref, view):
+            value = ref[...]
+            view[...] = jnp.transpose(jnp.concatenate([value, value], axis=0))
+            even = view[pl.ds(0, tiles, stride=2), :]
+            odd = view[pl.ds(1, tiles, stride=2), :]
+            return jnp.where(left, even, odd)
+
+        courant = by_tile(courant_ref, turned_ref)
+        scale = 1.0 / (1.0 + courant)
+        scale_ref[...] = scale
+        weight_ref[...] = courant * scale
+        slots_ref[...] = by_tile(slot_ref, index_ref) & (WIN - 1)
+
+    asides = {1: transport_weights, 2: scalar_products, 3: entry_weights}
 
     def arrival(d, m):
         source = lax.rem(flow + flow_count - d, flow_count)
@@ -237,6 +244,8 @@
                 device_id=others[m - 1],
                 device_id_type=MESH,
             ).start()
+        if d in asides:
+            asides[d]()
     for copy in mine:
         copy.wait()
     for d in range(1, flow_count):
@@ -453,8 +462,6 @@
         pair_ref[0, column(s)] = total
 
     def step(s, carry):
-        deposit(jnp.maximum(s - 1, 0))
-
         @pl.when(s == 1)
         def _():
             @pl.when(spot != 0)
@@ -471,6 +478,7 @@
 
         @pl.when(s >= 1)
         def _():
+            deposit(s - 1)
             hand_on(s - 1)
 
         base = column(s) * (per * deep)

time: 60.6 us -> 60.1 us (level)
    pallas_call x1, Pallas kernels: 32 us -> 31.3 us  [react(): pl.pallas_call(functools.partial(react_kernel, sizes), out_shape=jax.Shap...]
where the time goes in v4:
time: 60.1 us; the launch traced here: 59.9 us
  Pallas kernels  59.9 us (100%)
    pallas_call x1, Pallas kernels, react(): pl.pallas_call(functools.partial(react_kernel, sizes), out_shape=jax.Shap...  31.3 us
    pallas_call x1, Pallas kernels, forward(): pl.pallas_call(functools.partial(forward_kernel, sizes), out_shape=(jax.S...  26.6 us
    pallas_call x1, Pallas kernels, mean(): pl.pallas_call(mean_kernel, out_shape=jax.ShapeDtypeStruct((width, share...  2.03 us

profile of v4, /device:TPU:0, one launch (start us, length us, event | category | flops | bytes accessed | tf_op | source)
XLA Modules:
  0.0 59.9 jit_solution(1095893423881008215)
XLA Ops:
  0.0 26.6 %shard_map.100 = (f32[12,16384]{1,0:T(8,128)}, s32[128,128]{1,0:T(8,128)}, s32[128,128]{1,0:T(8,128)}, f32[128,128]{1,0:T(8,128)}, f32[128,128]{1,0:T(8,128)}, /*index=5*/f32[432]{0:T(512)}, bf16[624,240]{1,0:T(8,128)(2,1)}) custom-call(f32[6,12]{1,0:T(8,128)} %stoich_ref.3, f32[6,12]{1,0:T(8,128)} %stoich_ref.3, f32[624,12]{1,0:T(8,128)} %constant.6.clone.first_ref, ...), custom_call_target="tpu_custom_call" | custom-call | tf_op jit(solution)/shard_map/pallas_call | solution.py:277
  26.6 31.3 %shard_map.101.sums_ref = f32[4,304,128]{2,1,0:T(8,128)} custom-call(f32[6,12]{1,0:T(8,128)} %stoich_ref.3, f32[432]{0:T(512)} %get-tuple-element.12.pairs_ref, f32[6]{0:T(128)} %logk_ref.1, f32[12,16384]{1,0:T(8,128)} %get-tuple-element.13.cells_ref, s32[128,128]{1,0:T(8,128)} %get-tuple-element.14.pick_ref, s32[128,128]{1,0:T(8,128)} %get-tuple-element.15.slot_ref, ...), custom_call_target="tpu_custom_call" | custom-call | tf_op jit(solution)/shard_map/pallas_call | solution.py:554
  57.9 2.0 %shard_map.102 = f32[18,8192]{1,0:T(8,128)} custom-call(f32[4,304,128]{2,1,0:T(8,128)} %shard_map.101.sums_ref), custom_call_target="tpu_custom_call" | custom-call | tf_op jit(solution)/shard_map/pallas_call | solution.py:594

commit v5 on v4

--- a/solution.py
+++ b/solution.py
@@ -92,6 +92,14 @@
         logfree = [x - u for x, u in zip(logfree, update)]
     plex = [jnp.exp(logk[p] + blend(stoich[p], logfree)) for p in range(plexes)]
     return [jnp.exp(x) for x in logfree] + plex
+
+
+def partner(index, key, count):
+    total, weight = 0, 1
+    while weight < count:
+        total = total + weight * lax.rem(lax.div(index, weight) + key // weight % 2, 2)
+        weight *= 2
+    return total
 
 
 def forward_kernel(
@@ -129,7 +137,7 @@
     others = [
         (flow, lax.rem(rank + m, members) * parts + part) for m in range(1, members)
     ]
-    peers = [(lax.rem(flow + d, flow_count), group) for d in range(1, flow_count)]
+    peers = [(partner(flow, d, flow_count), group) for d in range(1, flow_count)]
     barrier = pltpu.get_barrier_semaphore()
     for peer in others + peers:
         pl.semaphore_signal(barrier, inc=1, device_id=peer, device_id_type=MESH)
@@ -219,7 +227,7 @@
     asides = {1: transport_weights, 2: scalar_products, 3: entry_weights}
 
     def arrival(d, m):
-        source = lax.rem(flow + flow_count - d, flow_count)
+        source = peers[d - 1][0]
         owner = lax.rem(rank + members - m, members)
         span = cut(source * capacity + owner * piece, piece)
         return pltpu.make_async_remote_copy(
@@ -233,7 +241,7 @@
 
     for d in range(1, flow_count):
         arrival(d, 0).wait_recv()
-        source = lax.rem(flow + flow_count - d, flow_count)
+        source = peers[d - 1][0]
         span = cut(source * capacity + rank * piece, piece)
         for m in range(1, members):
             pltpu.make_async_remote_copy(
@@ -249,7 +257,7 @@
     for copy in mine:
         copy.wait()
     for d in range(1, flow_count):
-        source = lax.rem(flow + flow_count - d, flow_count)
+        source = peers[d - 1][0]
         pltpu.make_async_remote_copy(
             src_ref=table_ref.at[rows(peers[d - 1][0])],
             dst_ref=picks_ref.at[rows(source)],
@@ -354,7 +362,7 @@
     place = lax.rem(flow, share)
 
     def column(s):
-        return lax.rem(flow + 1 + s, flow_count)
+        return partner(flow, flow_count - 1 - s, flow_count)
 
     def to_chief(s, index):
         return pltpu.make_async_remote_copy(

time: 60.1 us -> 60.3 us (level)
    pallas_call x1, Pallas kernels: 31.3 us -> 32.6 us  [react(): pl.pallas_call(functools.partial(react_kernel, sizes), out_shape=jax.Shap...]
    pallas_call x1, Pallas kernels: 26.6 us -> 25.4 us  [forward(): pl.pallas_call(functools.partial(forward_kernel, sizes), out_shape=(jax.S...]
where the time goes in v5:
time: 60.3 us; the launch traced here: 60.1 us
  Pallas kernels  60 us (100%)
    pallas_call x1, Pallas kernels, react(): pl.pallas_call(functools.partial(react_kernel, sizes), out_shape=jax.Shap...  32.6 us
    pallas_call x1, Pallas kernels, forward(): pl.pallas_call(functools.partial(forward_kernel, sizes), out_shape=(jax.S...  25.4 us
    pallas_call x1, Pallas kernels, mean(): pl.pallas_call(mean_kernel, out_shape=jax.ShapeDtypeStruct((width, share...  2.03 us

profile of v5, /device:TPU:0, one launch (start us, length us, event | category | flops | bytes accessed | tf_op | source)
XLA Modules:
  0.0 60.1 jit_solution(8442715710532322572)
XLA Ops:
  0.0 25.4 %shard_map.100 = (f32[12,16384]{1,0:T(8,128)}, s32[128,128]{1,0:T(8,128)}, s32[128,128]{1,0:T(8,128)}, f32[128,128]{1,0:T(8,128)}, f32[128,128]{1,0:T(8,128)}, /*index=5*/f32[432]{0:T(512)}, bf16[624,240]{1,0:T(8,128)(2,1)}) custom-call(f32[6,12]{1,0:T(8,128)} %stoich_ref.3, f32[6,12]{1,0:T(8,128)} %stoich_ref.3, f32[624,12]{1,0:T(8,128)} %constant.6.clone.first_ref, ...), custom_call_target="tpu_custom_call" | custom-call | tf_op jit(solution)/shard_map/pallas_call | solution.py:285
  25.4 32.6 %shard_map.101.sums_ref = f32[4,304,128]{2,1,0:T(8,128)} custom-call(f32[6,12]{1,0:T(8,128)} %stoich_ref.3, f32[432]{0:T(512)} %get-tuple-element.12.pairs_ref, f32[6]{0:T(128)} %logk_ref.1, f32[12,16384]{1,0:T(8,128)} %get-tuple-element.13.cells_ref, s32[128,128]{1,0:T(8,128)} %get-tuple-element.14.pick_ref, s32[128,128]{1,0:T(8,128)} %get-tuple-element.15.slot_ref, ...), custom_call_target="tpu_custom_call" | custom-call | tf_op jit(solution)/shard_map/pallas_call | solution.py:562
  58.0 2.0 %shard_map.102 = f32[18,8192]{1,0:T(8,128)} custom-call(f32[4,304,128]{2,1,0:T(8,128)} %shard_map.101.sums_ref), custom_call_target="tpu_custom_call" | custom-call | tf_op jit(solution)/shard_map/pallas_call | solution.py:602
